TPU v7x, 128 devices: a whole 4x4x4 slice. The times are simulated.
128 devices in a mesh: dp: 2 (over y_hi), ctx: 32 (over x, y_lo, z), head: 2 (over core).
Axes of the slice: x: 4, y: 4 (y_hi: 2, y_lo: 2; y = y_hi * 2 + y_lo), z: 4, core: 2. Of those that a mesh axis runs over, the one named last changes fastest.
Arguments:
- tokens: bfloat16 [16384, 768], P(('dp', 'ctx', 'head')), may hold values from -6 to 6
- first_gain: bfloat16 [768], P(('dp', 'ctx', 'head')), may hold values from 0.099609375 to 1.8984375
- first_shift: bfloat16 [768], P(('dp', 'ctx', 'head')), may hold values from -3 to 3
- second_gain: bfloat16 [768], P(('dp', 'ctx', 'head')), may hold values from 0.099609375 to 1.8984375
- second_shift: bfloat16 [768], P(('dp', 'ctx', 'head')), may hold values from -3 to 3
- qkv_weight: bfloat16 [768, 2304], P(('dp', 'ctx', 'head')), may hold values from -0.21875 to 0.21875
- out_weight: bfloat16 [768, 768], P(('dp', 'ctx', 'head')), may hold values from -0.875 to 0.875
- up_weight: bfloat16 [768, 3072], P(('dp', 'ctx', 'head')), may hold values from -0.21875 to 0.21875
- down_weight: bfloat16 [3072, 768], P(('dp', 'ctx', 'head')), may hold values from -0.109375 to 0.109375
- cotangent: bfloat16 [16384, 768], P(('dp', 'ctx', 'head')), may hold values from -6 to 6
Outputs:
- layer_out: bfloat16 [16384, 768], P(('dp', 'ctx', 'head'))
- tokens_grad: bfloat16 [16384, 768], P(('dp', 'ctx', 'head'))
- first_gain_grad: float32 [768], P(('dp', 'ctx', 'head'))
- first_shift_grad: float32 [768], P(('dp', 'ctx', 'head'))
- second_gain_grad: float32 [768], P(('dp', 'ctx', 'head'))
- second_shift_grad: float32 [768], P(('dp', 'ctx', 'head'))
- qkv_grad: float32 [768, 2304], P(('dp', 'ctx', 'head'))
- out_grad: float32 [768, 768], P(('dp', 'ctx', 'head'))
- up_grad: float32 [768, 3072], P(('dp', 'ctx', 'head'))
- down_grad: float32 [3072, 768], P(('dp', 'ctx', 'head'))
All inputs are finite; a program needn't handle non-finite values.
Results may differ from a plain program's by a relative error of at most 0.015.
Values may be sent and summed in bfloat16 or wider, within the bound.
No kernel may reach another device: no remote copies, remote signals or barrier semaphores. Data moves between devices by JAX's collectives and lax.ppermute only.
A program may use at most 256 MiB of HBM per device.

v0:
```python
import jax
import jax.numpy as jnp
from jax import lax
from jax.sharding import PartitionSpec as P

H = 12
HS = 64
ROT = 16


EPSILON = 1e-05


def layer_norm(values, gain_vec, shift_vec):
    middle = jnp.mean(values, axis=-1, keepdims=True)
    centred = values - middle
    spread = jnp.mean(centred * centred, axis=-1, keepdims=True)
    return centred * lax.rsqrt(spread + EPSILON) * gain_vec + shift_vec


def rotary_tables(positions, rot_dims):
    inverse = 1.0 / 10000.0 ** (jnp.arange(0, rot_dims, 2, dtype=jnp.float32) / rot_dims)
    angles = positions.astype(jnp.float32)[:, None] * inverse[None, :]
    angles = jnp.concatenate([angles, angles], axis=1)
    return (jnp.cos(angles), jnp.sin(angles))


def rotate_heads(values, cosine, sine_vals):
    half_dims = ROT // 2
    rotated_part = values[..., :ROT]
    turned_half = jnp.concatenate(
        [-rotated_part[..., half_dims:], rotated_part[..., :half_dims]], axis=-1
    )
    mixed = rotated_part * cosine[:, None, :] + turned_half * sine_vals[:, None, :]
    return jnp.concatenate([mixed, values[..., ROT:]], axis=-1)


def apply_rotary(flat_rows, cosine, sine_vals):
    row_count = flat_rows.shape[0]
    grouped = flat_rows.reshape(row_count, H, 3, HS)
    query_part = rotate_heads(grouped[:, :, 0], cosine, sine_vals)
    key_part = rotate_heads(grouped[:, :, 1], cosine, sine_vals)
    return jnp.stack([query_part, key_part, grouped[:, :, 2]], axis=2).reshape(
        row_count, H * 3 * HS
    )


def exact_gelu(values):
    return jax.nn.gelu(values, approximate=False)


def local(
    tokens,
    first_gain,
    first_shift,
    second_gain,
    second_shift,
    qkv_weight,
    out_weight,
    up_weight,
    down_weight,
    cotangent,
):
    gathered = (
        lax.all_gather(first_gain, ("dp", "ctx", "head"), axis=0, tiled=True),
        lax.all_gather(first_shift, ("dp", "ctx", "head"), axis=0, tiled=True),
        lax.all_gather(second_gain, ("dp", "ctx", "head"), axis=0, tiled=True),
        lax.all_gather(second_shift, ("dp", "ctx", "head"), axis=0, tiled=True),
        lax.all_gather(qkv_weight, ("dp", "ctx", "head"), axis=0, tiled=True),
        lax.all_gather(out_weight, ("dp", "ctx", "head"), axis=0, tiled=True),
        lax.all_gather(up_weight, ("dp", "ctx", "head"), axis=0, tiled=True),
        lax.all_gather(down_weight, ("dp", "ctx", "head"), axis=0, tiled=True),
    )
    gain_one, shift_one, gain_two, shift_two, qkv_full, out_full, up_full, down_full = gathered
    local_rows = tokens.shape[0]
    head_count = lax.axis_size("head")
    ctx_count = lax.axis_size("ctx")
    local_heads = H // head_count
    query_span = local_rows * head_count
    score_scale = HS ** (-0.5)
    rows_f32 = tokens.astype(jnp.float32)
    first_norm, first_pull = jax.vjp(
        layer_norm, rows_f32, gain_one.astype(jnp.float32), shift_one.astype(jnp.float32)
    )
    second_norm, second_pull = jax.vjp(
        layer_norm, rows_f32, gain_two.astype(jnp.float32), shift_two.astype(jnp.float32)
    )
    first_low = first_norm.astype(jnp.bfloat16)
    second_low = second_norm.astype(jnp.bfloat16)
    row_first = (lax.axis_index("ctx") * head_count + lax.axis_index("head")) * local_rows
    cosine, sine_vals = rotary_tables(row_first + jnp.arange(local_rows, dtype=jnp.int32), ROT)
    projected = jnp.dot(first_low, qkv_full, preferred_element_type=jnp.float32)
    turned, rotary_pull = jax.vjp(
        lambda flat_rows: apply_rotary(flat_rows, cosine, sine_vals), projected
    )
    head_rows = lax.all_to_all(
        turned.astype(jnp.bfloat16), "head", split_axis=1, concat_axis=0, tiled=True
    )
    grouped = head_rows.reshape(query_span, local_heads, 3, HS)
    queries = jnp.transpose(grouped[:, :, 0], (1, 0, 2))
    key_vals = grouped[:, :, 1:].reshape(query_span, local_heads * 2 * HS)
    query_first = lax.axis_index("ctx") * query_span
    query_places = query_first + jnp.arange(query_span, dtype=jnp.int32)
    query_last = query_first + query_span - 1

    def masked_scores(key_slab):
        slab_rows = key_slab.shape[0]
        paired = key_slab.reshape(slab_rows, local_heads, 2, HS)
        key_rows = paired[:, :, 0]
        value_rows = paired[:, :, 1]
        scores = (
            jnp.einsum("hqd,khd->hqk", queries, key_rows, preferred_element_type=jnp.float32)
            * score_scale
        )
        visible = jnp.arange(slab_rows, dtype=jnp.int32)[None, :] <= query_places[:, None]
        return (slab_rows, key_rows, value_rows, scores, visible[None])

    start_state = (
        jnp.full((local_heads, query_span), -1e30, jnp.float32),
        jnp.zeros((local_heads, query_span), jnp.float32),
        jnp.zeros((local_heads, query_span, HS), jnp.float32),
    )
    key_slab = lax.all_gather(key_vals, "ctx", axis=0, tiled=True)

    def forward_compute():
        row_peak, row_mass, weighted = start_state
        slab_rows, key_rows, value_rows, scores, visible = masked_scores(key_slab)
        new_peak = jnp.maximum(row_peak, jnp.max(jnp.where(visible, scores, -1e30), axis=-1))
        weights = jnp.where(visible, jnp.exp(scores - new_peak[..., None]), 0.0)
        new_mass = jnp.sum(weights, axis=-1)
        new_weighted = jnp.einsum(
            "hqk,khd->hqd",
            weights.astype(jnp.bfloat16),
            value_rows,
            preferred_element_type=jnp.float32,
        )
        return (new_peak, new_mass, new_weighted)

    row_peak, row_mass, weighted = lax.cond(
        jnp.int32(0) > query_last, lambda: start_state, forward_compute
    )
    log_mass = row_peak + jnp.log(row_mass)
    mixed = weighted / row_mass[..., None]
    heads_low = (
        jnp.transpose(mixed, (1, 0, 2)).reshape(query_span, local_heads * HS).astype(jnp.bfloat16)
    )
    token_heads = lax.all_to_all(heads_low, "head", split_axis=0, concat_axis=1, tiled=True)
    attended = jnp.dot(token_heads, out_full, preferred_element_type=jnp.float32)
    hidden = jnp.dot(second_low, up_full, preferred_element_type=jnp.float32)
    activated, gelu_pull = jax.vjp(exact_gelu, hidden)
    act_low = activated.astype(jnp.bfloat16)
    feed_out = jnp.dot(act_low, down_full, preferred_element_type=jnp.float32)
    layer_out = (rows_f32 + attended + feed_out).astype(jnp.bfloat16)
    cot_f32 = cotangent.astype(jnp.float32)
    out_w_grad = jnp.dot(token_heads.T, cotangent, preferred_element_type=jnp.float32)
    down_w_grad = jnp.dot(act_low.T, cotangent, preferred_element_type=jnp.float32)
    act_grad = jnp.dot(cotangent, down_full.T, preferred_element_type=jnp.float32)
    (hidden_grad,) = gelu_pull(act_grad)
    hidden_low = hidden_grad.astype(jnp.bfloat16)
    up_w_grad = jnp.dot(second_low.T, hidden_low, preferred_element_type=jnp.float32)
    second_in = jnp.dot(hidden_low, up_full.T, preferred_element_type=jnp.float32)
    second_rows, gain_two_grad, shift_two_grad = second_pull(second_in)
    heads_grad = jnp.dot(cotangent, out_full.T, preferred_element_type=jnp.float32).astype(
        jnp.bfloat16
    )
    grad_heads = lax.all_to_all(heads_grad, "head", split_axis=1, concat_axis=0, tiled=True)
    out_grads = jnp.transpose(grad_heads.reshape(query_span, local_heads, HS), (1, 0, 2))
    mixed_low = jnp.transpose(heads_low.reshape(query_span, local_heads, HS), (1, 0, 2))
    row_delta = jnp.sum(out_grads.astype(jnp.float32) * mixed_low.astype(jnp.float32), axis=-1)
    seq_length = query_span * ctx_count

    def slab_terms(key_slab):
        slab_rows, key_rows, value_rows, scores, visible = masked_scores(key_slab)
        weights = jnp.where(visible, jnp.exp(scores - log_mass[..., None]), 0.0)
        prob_grad = jnp.einsum(
            "hqd,khd->hqk", out_grads, value_rows, preferred_element_type=jnp.float32
        )
        score_grad = (weights * (prob_grad - row_delta[..., None])).astype(jnp.bfloat16)
        return (slab_rows, key_rows, weights, score_grad)

    query_zero = jnp.zeros((local_heads, query_span, HS), jnp.float32)
    back_state = (query_zero, jnp.zeros((seq_length, local_heads * 2 * HS), jnp.float32))
    backward_key_slab = lax.all_gather(key_vals, "ctx", axis=0, tiled=True)

    def backward_compute():
        slab_rows, key_rows, weights, score_grad = slab_terms(backward_key_slab)
        new_query = score_scale * jnp.einsum(
            "hqk,khd->hqd", score_grad, key_rows, preferred_element_type=jnp.float32
        )
        key_part = score_scale * jnp.einsum(
            "hqk,hqd->khd", score_grad, queries, preferred_element_type=jnp.float32
        )
        value_part = jnp.einsum(
            "hqk,hqd->khd",
            weights.astype(jnp.bfloat16),
            out_grads,
            preferred_element_type=jnp.float32,
        )
        block_grad = jnp.stack([key_part, value_part], axis=2).reshape(
            slab_rows, local_heads * 2 * HS
        )
        return (new_query, block_grad)

    back_result = lax.cond(jnp.int32(0) > query_last, lambda: back_state, backward_compute)
    query_grad = back_result[0]
    kv_mine = lax.psum_scatter(
        back_result[1].astype(jnp.bfloat16), "ctx", scatter_dimension=0, tiled=True
    ).astype(jnp.float32)
    kv_rows = kv_mine.reshape(query_span, local_heads, 2, HS)
    query_rows = jnp.transpose(query_grad, (1, 0, 2))[:, :, None, :]
    assembled = (
        jnp.concatenate([query_rows, kv_rows], axis=2)
        .reshape(query_span, local_heads * 3 * HS)
        .astype(jnp.bfloat16)
    )
    back_rows = lax.all_to_all(assembled, "head", split_axis=0, concat_axis=1, tiled=True)
    (pre_grad,) = rotary_pull(back_rows.astype(jnp.float32))
    pre_low = pre_grad.astype(jnp.bfloat16)
    qkv_w_grad = jnp.dot(first_low.T, pre_low, preferred_element_type=jnp.float32)
    first_in = jnp.dot(pre_low, qkv_full.T, preferred_element_type=jnp.float32)
    first_rows, gain_one_grad, shift_one_grad = first_pull(first_in)
    tokens_grad = (cot_f32 + first_rows + second_rows).astype(jnp.bfloat16)
    summed = (
        lax.psum_scatter(gain_one_grad, ("dp", "ctx", "head"), scatter_dimension=0, tiled=True),
        lax.psum_scatter(shift_one_grad, ("dp", "ctx", "head"), scatter_dimension=0, tiled=True),
        lax.psum_scatter(gain_two_grad, ("dp", "ctx", "head"), scatter_dimension=0, tiled=True),
        lax.psum_scatter(shift_two_grad, ("dp", "ctx", "head"), scatter_dimension=0, tiled=True),
        lax.psum_scatter(qkv_w_grad, ("dp", "ctx", "head"), scatter_dimension=0, tiled=True),
        lax.psum_scatter(out_w_grad, ("dp", "ctx", "head"), scatter_dimension=0, tiled=True),
        lax.psum_scatter(up_w_grad, ("dp", "ctx", "head"), scatter_dimension=0, tiled=True),
        lax.psum_scatter(down_w_grad, ("dp", "ctx", "head"), scatter_dimension=0, tiled=True),
    )
    gain_one_out, shift_one_out, gain_two_out, shift_two_out, qkv_out, out_out, up_out, down_out = (
        summed
    )
    return (
        layer_out,
        tokens_grad,
        gain_one_out,
        shift_one_out,
        gain_two_out,
        shift_two_out,
        qkv_out,
        out_out,
        up_out,
        down_out,
    )


def solution(mesh):
    in_specs = (
        P(("dp", "ctx", "head"), None),
        P(("dp", "ctx", "head")),
        P(("dp", "ctx", "head")),
        P(("dp", "ctx", "head")),
        P(("dp", "ctx", "head")),
        P(("dp", "ctx", "head"), None),
        P(("dp", "ctx", "head"), None),
        P(("dp", "ctx", "head"), None),
        P(("dp", "ctx", "head"), None),
        P(("dp", "ctx", "head"), None),
    )
    out_specs = (
        P(("dp", "ctx", "head"), None),
        P(("dp", "ctx", "head"), None),
        P(("dp", "ctx", "head")),
        P(("dp", "ctx", "head")),
        P(("dp", "ctx", "head")),
        P(("dp", "ctx", "head")),
        P(("dp", "ctx", "head"), None),
        P(("dp", "ctx", "head"), None),
        P(("dp", "ctx", "head"), None),
        P(("dp", "ctx", "head"), None),
    )
    return jax.shard_map(local, mesh=mesh, in_specs=in_specs, out_specs=out_specs, check_vma=False)
```

profile of v0, /device:TPU:2, one launch (start us, length us, event | category | flops | bytes accessed | tf_op | source)
XLA Modules:
  0.0 2045.4 jit_solution(11620263486823284853)
XLA Ops:
  12.2 67.4 %all-reduce.26 = (bf16[768]{0:T(1024)(128)(2,1)}, bf16[768]{0:T(1024)(128)(2,1)}, bf16[768]{0:T(1024)(128)(2,1)S(1)}, bf16[768]{0:T(1024)(128)(2,1)S(1)}) all-reduce(bf16[768]{0:T(1024)(128)(2,1)S(1)} %dynamic-update-slice.3, bf16[768]{0:T(1024)(128)(2,1)S(1)} %dynamic-update-slice.2, ...), channel_id=1, replica_groups=mesh['dp'=2,'ctx'=32,'head'=2] {'dp','ctx','head'}, use_global_device_ids=true, to_apply=%add.14 | all-reduce | flops 3072 | bytes 12288
  83.9 127.5 %all-gather.13.cloned.1.call-done = bf16[128,6,2304]{2,1,0:T(8,128)(2,1)} async-done(((bf16[1,6,2304]{2,1,0:T(8,128)(2,1)}), bf16[128,6,2304]{2,1,0:T(8,128)(2,1)}) %all-gather.13.cloned.1.call-update) | async-done | bytes 3538960 | tf_op jit(solution)/shard_map/all_gather | solution.py:69
  211.4 5.0 reshape.243
  219.8 4.2 all_to_all.55
  224.0 4.9 copy.74
  231.3 173.8 %all-gather.15.cloned.1.call-done = bf16[128,6,768]{2,1,0:T(8,128)(2,1)} async-done(((bf16[1,6,768]{2,1,0:T(8,128)(2,1)}), bf16[128,6,768]{2,1,0:T(8,128)(2,1)}) %all-gather.15.cloned.1.call-update) | async-done | bytes 1179664 | tf_op jit(solution)/shard_map/all_gather | solution.py:70
  408.0 4.1 all_to_all.56
  413.3 198.5 %all-gather.9.cloned.1.call-done = bf16[8192,768]{0,1:T(8,128)(2,1)} async-done(((bf16[256,768]{0,1:T(8,128)(2,1)}), bf16[8192,768]{0,1:T(8,128)(2,1)}) %all-gather.9.cloned.1.call-update) | async-done | bytes 12582928 | tf_op jit(solution)/shard_map/all_gather | solution.py:123
  611.7 65.6 %conditional.2 = (f32[6,256]{1,0:T(8,128)S(1)}, f32[6,256]{1,0:T(8,128)S(1)}, f32[6,256]{1,0:T(8,128)S(1)}, f32[6,256,64]{2,1,0:T(8,128)S(1)}) conditional(s32[]{:T(128)} %convert_element_type.108, (s32[256]{0:T(256)S(1)}, bf16[8192,768]{0,1:T(8,128)(2,1)}, bf16[6,256,64]{1,2,0:T(8,128)(2,1)S(1)}) %tuple.26, () %tuple.27), branch_computations={%region_2.5_spmd, %region_5.0_spmd} | conditional | flops 3361733120 | bytes 172606496 | solution.py:139
  613.0 21.2 %select_reduce_fusion = (f32[6,256]{1,0:T(8,128)S(1)}, f32[6,256,8192]{2,1,0:T(8,128)}) fusion(pred[256,8192]{1,0:T(8,128)(4,1)S(1)} %iota_compare_fusion, bf16[6,256,64]{1,2,0:T(8,128)(2,1)S(1)} %get-tuple-element.28, bf16[8192,6,2,64]{0,3,2,1:T(8,128)(2,1)} %bitcast.132), kind=kOutput, calls=%fused_computation.1 | convolution fusion | flops 1648359936 | bytes 58923008 | tf_op jit(solution)/shard_map/cond/branch_0_fun/hqd,khd->hqk/dot_general | solution.py:112
  634.2 22.9 %fusion.4 = f32[6,256]{1,0:T(8,128)S(1)} fusion(f32[6,256,8192]{2,1,0:T(8,128)} %get-tuple-element.98, f32[6,256]{1,0:T(8,128)S(1)} %broadcast_maximum_fusion, pred[256,8192]{1,0:T(8,128)(4,1)S(1)} %iota_compare_fusion), kind=kLoop, calls=%fused_computation.3 | loop fusion | flops 50330112 | bytes 52441088 | tf_op jit(solution)/shard_map/cond/branch_0_fun/reduce_sum | solution.py:130
  657.2 20.2 fusion.5
  678.4 116.7 %conditional.3 = (bf16[6,256,64]{1,2,0:T(8,128)(2,1)}, bf16[8192,768]{0,1:T(8,128)(2,1)}) conditional(s32[]{:T(128)} %convert_element_type.108, (s32[256]{0:T(256)S(1)}, bf16[8192,768]{0,1:T(8,128)(2,1)}, bf16[6,256,64]{1,2,0:T(8,128)(2,1)S(1)}, f32[6,256]{1,0:T(8,128)S(1)}, f32[6,256]{1,0:T(8,128)S(1)}, /*index=5*/bf16[6,256,64]{1,2,0:T(8,128)(2,1)}, ...), branch_computations={%region_6.8_spmd, %region_8.9_spmd} | conditional | flops 8193966080 | bytes 319532096 | solution.py:204
  678.4 21.8 %fusion.19 = f32[6,256,8192]{2,1,0:T(8,128)} fusion(bf16[6,256,64]{1,2,0:T(8,128)(2,1)S(1)} %get-tuple-element.31, bf16[8192,6,2,64]{0,3,2,1:T(8,128)(2,1)} %bitcast.134), kind=kOutput, calls=%fused_computation.25 | convolution fusion | flops 1610612736 | bytes 56819712 | tf_op jit(solution)/shard_map/cond/branch_0_fun/hqd,khd->hqk/dot_general | solution.py:112
  702.1 33.1 %multiply_convert_fusion = bf16[6,256,8192]{2,1,0:T(8,128)(2,1)} fusion(f32[6,256,8192]{2,1,0:T(8,128)} %fusion.19, f32[6,256]{1,0:T(8,128)S(1)} %multiply_reduce_fusion, f32[6,256]{1,0:T(8,128)S(1)} %add.75, pred[256,8192]{1,0:T(8,128)(4,1)S(1)} %iota_compare_fusion.1, bf16[6,256,64]{1,2,0:T(8,128)(2,1)S(1)} %copy-done.16, ...), kind=kOutput, calls=%fused_computation.13 | convolution fusion | flops 1686110208 | bytes 84094976 | tf_op jit(solution)/shard_map/cond/branch_0_fun/hqd,khd->hqk/dot_general | solution.py:175
  735.2 14.1 fusion.20
  749.4 23.0 %fusion.15 = bf16[8192,6,1,64]{0,3,1,2:T(8,128)(2,1)} fusion(bf16[6,256,64]{1,2,0:T(8,128)(2,1)S(1)} %copy-done.16, f32[6,256,8192]{2,1,0:T(8,128)} %fusion.19, f32[6,256]{1,0:T(8,128)S(1)} %add.75, pred[256,8192]{1,0:T(8,128)(4,1)S(1)} %iota_compare_fusion.1), kind=kOutput, calls=%fused_computation.20 | convolution fusion | flops 1660944384 | bytes 58923008 | tf_op jit(solution)/shard_map/cond/branch_0_fun/hqk,hqd->khd/dot_general | solution.py:193
  772.4 12.7 multiply_bitcast_fusion
  785.1 4.8 pad_maximum_fusion
  789.9 5.2 copy.70
  795.8 20.3 all-gather.17.cloned.1.call-done
  816.2 7.8 reshape.247
  823.9 3.3 fusion.59
  827.2 188.7 %all-gather.11.cloned.1.call-done = bf16[3072,768]{1,0:T(8,128)(2,1)} async-done(((bf16[24,768]{1,0:T(8,128)(2,1)}), bf16[3072,768]{1,0:T(8,128)(2,1)}) %all-gather.11.cloned.1.call-update) | async-done | bytes 4718608 | tf_op jit(solution)/shard_map/all_gather | solution.py:72
  1015.9 6.3 add_convert_fusion
  1022.4 5.0 fusion.78
  1027.4 5.1 fusion.57
  1032.7 3.9 all_to_all.57
  1037.8 153.8 %reduce-scatter.9.cloned.1.call-done = bf16[256,768]{0,1:T(8,128)(2,1)} async-done(((bf16[8192,768]{0,1:T(8,128)(2,1)}), bf16[256,768]{0,1:T(8,128)(2,1)}) %reduce-scatter.9.cloned.1.call-update) | async-done | bytes 393232 | tf_op jit(solution)/shard_map/reduce_scatter | solution.py:206
  1197.1 4.4 all_to_all.58
  1203.3 4.1 fusion.61
  1207.4 327.4 %fusion.71 = (f32[8,2304]{1,0:T(8,128)}, f32[8,768]{1,0:T(8,128)}, f32[8,3072]{1,0:T(8,128)}) fusion(f32[768,2304]{1,0:T(8,128)} %fusion.61, f32[768,768]{1,0:T(8,128)S(1)} %fusion.77, f32[768,3072]{1,0:T(8,128)} %fusion.57), kind=kCustom, calls=%all-reduce-scatter.3 | all-reduce-scatter fusion | flops 6291457 | bytes 19070976
  1542.2 18.4 collective-permute-start.58
  1560.6 47.7 %collective-permute-start.57 = (f32[8,768]{1,0:T(8,128)}, f32[8,768]{1,0:T(8,128)S(1)}, u32[]{:S(2)}, u32[]{:S(2)}) collective-permute-start(f32[8,768]{1,0:T(8,128)} %get-tuple-element.91), channel_id=1, source_target_pairs={{0,26},{1,27},{2,28},{3,29},{4,30},{5,31},{6,32},{7,33},{8,34},{9,... | collective-permute-start | bytes 73736
  1608.4 3.4 collective-permute-start.56
  1611.9 5.1 collective-permute-start.55
  1617.0 4.4 collective-permute-start.54
  1630.2 3.6 collective-permute-start.48
  1635.8 5.3 collective-permute-start.46
  1665.4 3.8 collective-permute-start.35
  1682.1 5.9 collective-permute-done.33
  1689.9 6.7 collective-permute-done.32
  1704.0 4.3 fusion.76
  1708.3 6.0 collective-permute-start.22
  1722.9 3.1 fusion.75
  1753.9 4.6 collective-permute-start.6
  1762.9 4.3 collective-permute-start.3
  1778.5 4.5 collective-permute-done.1
  1795.6 5.2 collective-permute-start.86
  1800.8 4.9 collective-permute-start.85
  1805.7 3.3 collective-permute-start.84
  1809.1 3.8 collective-permute-start.83
  1818.9 4.8 collective-permute-start.78
  1823.7 5.2 collective-permute-start.77
  1832.0 4.6 collective-permute-start.75
  1839.6 64.5 %all-reduce.25 = (f32[768]{0:T(1024)S(1)}, f32[768]{0:T(1024)S(1)}, f32[768]{0:T(1024)S(1)}, f32[768]{0:T(1024)S(1)}) all-reduce(f32[768]{0:T(1024)S(1)} %get-tuple-element.78, f32[768]{0:T(1024)} %get-tuple-element.75, f32[768]{0:T(1024)S(1)} %get-tuple-element.69, ...), channel_id=3, replica_groups=mesh['dp'=2,'ctx'=32,'head'=2] {'dp','ctx','head'}, use_global_device_ids=true, to_apply=%region_15.16.clone | all-reduce | flops 3072 | bytes 24576
  1906.4 26.5 %concatenate.36 = f32[262,768]{1,0:T(8,128)S(1)} concatenate(f32[6,768]{1,0:T(8,128)} %copy-done.93, f32[8,768]{1,0:T(8,128)S(1)} %copy-done.91, f32[8,768]{1,0:T(8,128)} %copy-done.92, f32[8,768]{1,0:T(8,128)} %copy-done.94, f32[8,768]{1,0:T(8,128)} %copy-done.95, f32[8,768]{1,0:T(8,128)} %copy-done.96, f32[8,768]{1,0:T(8,128)} %copy-done.97, f32[8,768]{1,0:T(8,128)} %copy-done.98, ...), dimensions={0} | concatenate | bytes 1609728
  1934.9 3.3 collective-permute-start.72
  1941.1 4.9 collective-permute-start.70
  1946.0 4.0 collective-permute-start.69
  1950.8 32.6 %concatenate.35 = f32[262,2304]{1,0:T(8,128)S(1)} concatenate(f32[6,2304]{1,0:T(8,128)} %copy-done.58, f32[8,2304]{1,0:T(8,128)} %copy-done.55, f32[8,2304]{1,0:T(8,128)} %copy-done.56, f32[8,2304]{1,0:T(8,128)} %copy-done.57, f32[8,2304]{1,0:T(8,128)} %copy-done.59, f32[8,2304]{1,0:T(8,128)} %copy-done.60, f32[8,2304]{1,0:T(8,128)} %copy-done.61, f32[8,2304]{1,0:T(8,128)} %copy-done.62, ...), dimensions={0} | concatenate | bytes 4829184
  1985.4 5.9 collective-permute-start.67
  1993.3 3.5 collective-permute-start.65
  2005.9 31.5 %concatenate.37 = f32[262,3072]{1,0:T(8,128)S(1)} concatenate(f32[6,3072]{1,0:T(8,128)} %copy-done.24, f32[8,3072]{1,0:T(8,128)} %copy-done.23, f32[8,3072]{1,0:T(8,128)} %copy-done.25, f32[8,3072]{1,0:T(8,128)} %copy-done.26, f32[8,3072]{1,0:T(8,128)} %copy-done.27, f32[8,3072]{1,0:T(8,128)} %copy-done.28, f32[8,3072]{1,0:T(8,128)} %copy-done.29, f32[8,3072]{1,0:T(8,128)S(1)} %copy-done.31, ...), dimensions={0} | concatenate | bytes 6438912
  (521 shorter events, 193.0 us)
Async XLA Ops:
  7.2 204.3 %all-gather.13.cloned.1.call-start = ((), (), s32[]{:S(2)}) async-start(), calls=%async_computation.10 | async-start | bytes 4755456 | tf_op jit(solution)/shard_map/all_gather | solution.py:69
  7.9 397.2 %all-gather.15.cloned.1.call-start = ((), (), s32[]{:S(2)}) async-start(), calls=%async_computation.11 | async-start | bytes 1585152 | tf_op jit(solution)/shard_map/all_gather | solution.py:70
  8.7 603.1 %all-gather.9.cloned.1.call-start = ((), (), s32[]{:S(2)}) async-start(), calls=%async_computation.6 | async-start | bytes 12976128 | tf_op jit(solution)/shard_map/all_gather | solution.py:123
  230.0 586.1 %all-gather.17.cloned.1.call-start = ((), (), s32[]{:S(2)}) async-start(), calls=%async_computation.12 | async-start | bytes 6340608 | tf_op jit(solution)/shard_map/all_gather | solution.py:71
  230.6 785.3 %all-gather.11.cloned.1.call-start = ((), (), s32[]{:S(2)}) async-start(), calls=%async_computation.7 | async-start | bytes 4755456 | tf_op jit(solution)/shard_map/all_gather | solution.py:72
  231.2 960.3 %reduce-scatter.9.cloned.1.call-start = ((), (), s32[]{:S(2)}) async-start(), calls=%async_computation.8 | async-start | bytes 12976128 | tf_op jit(solution)/shard_map/reduce_scatter | solution.py:206
  795.1 1242.9 %reduce-scatter.11.cloned.1.call-start = ((), (), s32[]{:S(2)}) async-start(), calls=%async_computation.9 | async-start | bytes 9510912 | tf_op jit(solution)/shard_map/reduce_scatter | solution.py:231
  1534.8 25.8 %collective-permute-start.62 = (f32[8,768]{1,0:T(8,128)}, f32[8,768]{1,0:T(8,128)S(1)}, u32[]{:S(2)}, u32[]{:S(2)}) collective-permute-start(f32[8,768]{1,0:T(8,128)} %get-tuple-element.91), channel_id=1, source_target_pairs={{0,31},{1,32},{2,33},{3,34},{4,35},{5,36},{6,37},{7,38},{8,39},{9,... | collective-permute-start | bytes 73736
  1536.3 72.1 %collective-permute-start.61 = (f32[8,768]{1,0:T(8,128)}, f32[8,768]{1,0:T(8,128)S(1)}, u32[]{:S(2)}, u32[]{:S(2)}) collective-permute-start(f32[8,768]{1,0:T(8,128)} %get-tuple-element.91), channel_id=1, source_target_pairs={{0,30},{1,31},{2,32},{3,33},{4,34},{5,35},{6,36},{7,37},{8,38},{9,... | collective-permute-start | bytes 73736
  1539.6 72.2 %collective-permute-start.60 = (f32[8,768]{1,0:T(8,128)}, f32[8,768]{1,0:T(8,128)S(1)}, u32[]{:S(2)}, u32[]{:S(2)}) collective-permute-start(f32[8,768]{1,0:T(8,128)} %get-tuple-element.91), channel_id=1, source_target_pairs={{0,29},{1,30},{2,31},{3,32},{4,33},{5,34},{6,35},{7,36},{8,37},{9,... | collective-permute-start | bytes 73736
  1540.9 76.1 %collective-permute-start.59 = (f32[8,768]{1,0:T(8,128)}, f32[8,768]{1,0:T(8,128)S(1)}, u32[]{:S(2)}, u32[]{:S(2)}) collective-permute-start(f32[8,768]{1,0:T(8,128)} %get-tuple-element.91), channel_id=1, source_target_pairs={{0,28},{1,29},{2,30},{3,31},{4,32},{5,33},{6,34},{7,35},{8,36},{9,... | collective-permute-start | bytes 73736
  1542.2 79.2 %collective-permute-start.58 = (f32[8,768]{1,0:T(8,128)}, f32[8,768]{1,0:T(8,128)S(1)}, u32[]{:S(2)}, u32[]{:S(2)}) collective-permute-start(f32[8,768]{1,0:T(8,128)} %get-tuple-element.91), channel_id=1, source_target_pairs={{0,27},{1,28},{2,29},{3,30},{4,31},{5,32},{6,33},{7,34},{8,35},{9,... | collective-permute-start | bytes 73736
  1560.6 62.1 %collective-permute-start.57 = (f32[8,768]{1,0:T(8,128)}, f32[8,768]{1,0:T(8,128)S(1)}, u32[]{:S(2)}, u32[]{:S(2)}) collective-permute-start(f32[8,768]{1,0:T(8,128)} %get-tuple-element.91), channel_id=1, source_target_pairs={{0,26},{1,27},{2,28},{3,29},{4,30},{5,31},{6,32},{7,33},{8,34},{9,... | collective-permute-start | bytes 73736
  1608.4 15.6 collective-permute-start.56
  1611.9 13.5 collective-permute-start.55
  1625.4 15.7 collective-permute-start.50
  1627.4 15.7 collective-permute-start.49
  1630.2 14.8 collective-permute-start.48
  1635.8 14.1 collective-permute-start.46
  1654.6 14.5 collective-permute-start.39
  1657.8 13.4 collective-permute-start.38
  1671.2 28.0 %collective-permute-start.30 = (f32[8,2304]{1,0:T(8,128)}, f32[8,2304]{1,0:T(8,128)S(1)}, u32[]{:S(2)}, u32[]{:S(2)}) collective-permute-start(f32[8,2304]{1,0:T(8,128)} %get-tuple-element.90), channel_id=1, source_target_pairs={{0,31},{1,32},{2,33},{3,34},{4,35},{5,36},{6,37},{7,38},{8,39},{9,... | collective-permute-start | bytes 221192
  1673.1 27.4 %collective-permute-start.29 = (f32[8,2304]{1,0:T(8,128)}, f32[8,2304]{1,0:T(8,128)S(1)}, u32[]{:S(2)}, u32[]{:S(2)}) collective-permute-start(f32[8,2304]{1,0:T(8,128)} %get-tuple-element.90), channel_id=1, source_target_pairs={{0,30},{1,31},{2,32},{3,33},{4,34},{5,35},{6,36},{7,37},{8,38},{9,... | collective-permute-start | bytes 221192
  1674.5 27.4 %collective-permute-start.28 = (f32[8,2304]{1,0:T(8,128)}, f32[8,2304]{1,0:T(8,128)S(1)}, u32[]{:S(2)}, u32[]{:S(2)}) collective-permute-start(f32[8,2304]{1,0:T(8,128)} %get-tuple-element.90), channel_id=1, source_target_pairs={{0,29},{1,30},{2,31},{3,32},{4,33},{5,34},{6,35},{7,36},{8,37},{9,... | collective-permute-start | bytes 221192
  1677.7 20.2 collective-permute-start.31
  1697.9 16.4 collective-permute-start.26
  1699.2 17.5 collective-permute-start.25
  1700.6 18.1 collective-permute-start.24
  1702.5 18.4 collective-permute-start.23
  1708.3 17.8 collective-permute-start.22
  1730.8 13.7 collective-permute-start.14
  1733.8 13.4 collective-permute-start.13
  1737.3 14.6 collective-permute-start.12
  1740.0 13.9 collective-permute-start.11
  1742.0 16.5 collective-permute-start.10
  1744.5 16.2 collective-permute-start.9
  1747.3 15.6 collective-permute-start.8
  1751.9 15.4 collective-permute-start.7
  1753.9 15.4 collective-permute-start.6
  1760.7 13.4 collective-permute-start.4
  1769.3 13.6 collective-permute-start.1
  1771.5 14.7 collective-permute-start
  1774.1 14.7 collective-permute-start.94
  1777.2 13.8 collective-permute-start.93
  1788.8 16.9 collective-permute-start.89
  1791.1 18.0 collective-permute-start.88
  1793.2 19.7 collective-permute-start.87
  1795.6 18.7 collective-permute-start.86
  1800.8 14.8 collective-permute-start.85
  1814.2 14.7 collective-permute-start.81
  1815.6 16.4 collective-permute-start.80
  1816.9 19.7 collective-permute-start.79
  1818.9 114.1 %collective-permute-start.78 = (f32[8,3072]{1,0:T(8,128)S(1)}, f32[8,3072]{1,0:T(8,128)S(1)}, u32[]{:S(2)}, u32[]{:S(2)}) collective-permute-start(f32[8,3072]{1,0:T(8,128)S(1)} %copy-done.14), channel_id=1, source_target_pairs={{0,15},{1,16},{2,17},{3,18},{4,19},{5,20},{6,21},{7,22},{8,23},{9,... | collective-permute-start | bytes 294920
  1823.7 111.2 %collective-permute-start.77 = (f32[8,3072]{1,0:T(8,128)S(1)}, f32[8,3072]{1,0:T(8,128)S(1)}, u32[]{:S(2)}, u32[]{:S(2)}) collective-permute-start(f32[8,3072]{1,0:T(8,128)S(1)} %copy-done.14), channel_id=1, source_target_pairs={{0,14},{1,15},{2,16},{3,17},{4,18},{5,19},{6,20},{7,21},{8,22},{9,... | collective-permute-start | bytes 294920
  1828.9 109.3 %collective-permute-start.76 = (f32[8,3072]{1,0:T(8,128)S(1)}, f32[8,3072]{1,0:T(8,128)S(1)}, u32[]{:S(2)}, u32[]{:S(2)}) collective-permute-start(f32[8,3072]{1,0:T(8,128)S(1)} %copy-done.14), channel_id=1, source_target_pairs={{0,13},{1,14},{2,15},{3,16},{4,17},{5,18},{6,19},{7,20},{8,21},{9,... | collective-permute-start | bytes 294920
  1832.0 109.1 %collective-permute-start.75 = (f32[8,3072]{1,0:T(8,128)S(1)}, f32[8,3072]{1,0:T(8,128)S(1)}, u32[]{:S(2)}, u32[]{:S(2)}) collective-permute-start(f32[8,3072]{1,0:T(8,128)S(1)} %copy-done.14), channel_id=1, source_target_pairs={{0,12},{1,13},{2,14},{3,15},{4,16},{5,17},{6,18},{7,19},{8,20},{9,... | collective-permute-start | bytes 294920
  1836.6 109.4 %collective-permute-start.74 = (f32[8,3072]{1,0:T(8,128)S(1)}, f32[8,3072]{1,0:T(8,128)S(1)}, u32[]{:S(2)}, u32[]{:S(2)}) collective-permute-start(f32[8,3072]{1,0:T(8,128)S(1)} %copy-done.14), channel_id=1, source_target_pairs={{0,11},{1,12},{2,13},{3,14},{4,15},{5,16},{6,17},{7,18},{8,19},{9,... | collective-permute-start | bytes 294920
  1933.0 50.5 %collective-permute-start.73 = (f32[8,3072]{1,0:T(8,128)S(1)}, f32[8,3072]{1,0:T(8,128)}, u32[]{:S(2)}, u32[]{:S(2)}) collective-permute-start(f32[8,3072]{1,0:T(8,128)S(1)} %copy-done.14), channel_id=1, source_target_pairs={{0,10},{1,11},{2,12},{3,13},{4,14},{5,15},{6,16},{7,17},{8,18},{9,... | collective-permute-start | bytes 294920
  1934.9 50.5 %collective-permute-start.72 = (f32[8,3072]{1,0:T(8,128)S(1)}, f32[8,3072]{1,0:T(8,128)}, u32[]{:S(2)}, u32[]{:S(2)}) collective-permute-start(f32[8,3072]{1,0:T(8,128)S(1)} %copy-done.14), channel_id=1, source_target_pairs={{0,9},{1,10},{2,11},{3,12},{4,13},{5,14},{6,15},{7,16},{8,17},{9,1... | collective-permute-start | bytes 294920
  1938.3 53.0 %collective-permute-start.71 = (f32[8,3072]{1,0:T(8,128)S(1)}, f32[8,3072]{1,0:T(8,128)}, u32[]{:S(2)}, u32[]{:S(2)}) collective-permute-start(f32[8,3072]{1,0:T(8,128)S(1)} %copy-done.14), channel_id=1, source_target_pairs={{0,8},{1,9},{2,10},{3,11},{4,12},{5,13},{6,14},{7,15},{8,16},{9,17... | collective-permute-start | bytes 294920
  1941.1 52.2 %collective-permute-start.70 = (f32[8,3072]{1,0:T(8,128)S(1)}, f32[8,3072]{1,0:T(8,128)}, u32[]{:S(2)}, u32[]{:S(2)}) collective-permute-start(f32[8,3072]{1,0:T(8,128)S(1)} %copy-done.14), channel_id=1, source_target_pairs={{0,7},{1,8},{2,9},{3,10},{4,11},{5,12},{6,13},{7,14},{8,15},{9,16}... | collective-permute-start | bytes 294920
  1946.0 50.8 %collective-permute-start.69 = (f32[8,3072]{1,0:T(8,128)S(1)}, f32[8,3072]{1,0:T(8,128)}, u32[]{:S(2)}, u32[]{:S(2)}) collective-permute-start(f32[8,3072]{1,0:T(8,128)S(1)} %copy-done.14), channel_id=1, source_target_pairs={{0,6},{1,7},{2,8},{3,9},{4,10},{5,11},{6,12},{7,13},{8,14},{9,15},... | collective-permute-start | bytes 294920
  1983.5 16.6 collective-permute-start.68
  1985.4 14.6 collective-permute-start.67
  (166 other events, 7629.8 us)
Sparse Core Ops, SparseCore 0:
  9.7 201.6 all-gather.12
  213.2 191.9 all-gather.14
  406.7 204.9 all-gather.8
  613.3 202.7 all-gather.16
  817.7 198.1 all-gather.10
  1018.1 173.3 reduce-scatter.8
  1194.5 619.0 reduce-scatter.10
where the time goes:
time: 2060 us; the launch traced here: 2050 us
  waiting for transfers between devices  890 us (43%)
  blocking collectives  476 us (23%)
  starting transfers between devices  301 us (15%)
  matrix products  184 us (9%)
  local copies, waits for them, and re-layouts  137 us (7%)
  other arithmetic  39.8 us (2%)
    unnamed x3, blocking collectives  459 us
    unnamed x96, starting transfers between devices  300 us
    all_gather x1, waiting for transfers between devices, local(): key_slab = lax.all_gather(key_vals, 'ctx', axis=0, tiled=True)  198 us
    all_gather x1, waiting for transfers between devices, local(): lax.all_gather(down_weight, ('dp', 'ctx', 'head'), axis=0, tiled=True)  189 us
    all_gather x1, waiting for transfers between devices, local(): lax.all_gather(out_weight, ('dp', 'ctx', 'head'), axis=0, tiled=True)  174 us
    reduce_scatter x1, waiting for transfers between devices, local(): lax.psum_scatter(back_result[1].astype(jnp.bfloat16), 'ctx', scatter_dime...  154 us
    all_gather x1, waiting for transfers between devices, local(): lax.all_gather(qkv_weight, ('dp', 'ctx', 'head'), axis=0, tiled=True)  127 us
    unnamed x275, local copies, waits for them, and re-layouts  121 us
  transfers between devices with their start and end apart: 103, of which 14 were waited for; matrix products, arithmetic and copies ran while one was open for 33% of the time, Pallas kernels for 0%

commit v1 on v0

v1 whole, which is shorter than its diff:
```python
import functools

import jax
import jax.numpy as jnp
from jax import lax
from jax.experimental import pallas as pl
from jax.experimental.pallas import tpu as pltpu
from jax.sharding import Mesh, PartitionSpec as P

H = 12
HS = 64
ROT = 16
D = 768
FF = 3072
EPSILON = 1e-05
BF = jnp.bfloat16
F32 = jnp.float32
CHIPS = ("dp", "x", "y", "z")
ALL = ("dp", "x", "y", "z", "c")
GH = 3
QN = 512
NB = 16


def layer_norm(values, gain_vec, shift_vec):
    middle = jnp.mean(values, axis=-1, keepdims=True)
    centred = values - middle
    spread = jnp.mean(centred * centred, axis=-1, keepdims=True)
    return centred * lax.rsqrt(spread + EPSILON) * gain_vec + shift_vec


def exact_gelu(values):
    return jax.nn.gelu(values, approximate=False)


def dot(a, b, dims=((1,), (0,))):
    return lax.dot_general(a, b, (dims, ((), ())), preferred_element_type=F32)


def attn_kernel(qd_ref, kv_ref, oq_ref, dkv_ref, kt_ref):
    x = lax.axis_index("x")
    z = lax.axis_index("z")
    qd = qd_ref[...]
    lane = lax.broadcasted_iota(jnp.int32, (QN, 128), 1)
    zero = jnp.zeros_like(qd)
    q0 = jnp.where(lane < HS, qd, zero)
    do0 = jnp.where(lane >= HS, qd, zero)
    q_t = q0.astype(F32).T.astype(BF)
    do_f = do0.astype(F32).T
    do_t = do_f.astype(BF)
    col = lax.broadcasted_iota(jnp.int32, (1, QN), 1)
    q_place = (col // 256) * 1024 + z * 256 + col % 256
    krow = lax.broadcasted_iota(jnp.int32, (QN, 1), 0)
    k_place = (krow // 256) * 1024 + krow % 256

    def fwd(b, carry, masked):
        m, l, acc = carry
        start = pl.multiple_of(b * QN, QN)
        k = kv_ref[pl.ds(start, QN), :]
        k_t = k.astype(F32).T.astype(BF)
        kt_ref[b] = k_t
        s = dot(k, q_t)
        if masked:
            s = jnp.where(k_place + (b % 4) * 256 <= q_place, s, -1e30)
        m_new = jnp.maximum(m, jnp.max(s, axis=0, keepdims=True))
        p = jnp.exp(s - m_new)
        alpha = jnp.exp(m - m_new)
        l = l * alpha + jnp.sum(p, axis=0, keepdims=True)
        acc = acc * alpha + dot(k_t, p.astype(BF))
        return m_new, l, acc

    carry = (
        jnp.full((1, QN), -1e30, F32),
        jnp.zeros((1, QN), F32),
        jnp.zeros((128, QN), F32),
    )
    carry = lax.fori_loop(0, 4 * x, functools.partial(fwd, masked=False), carry)
    m, l, acc = lax.fori_loop(4 * x, 4 * x + 4, functools.partial(fwd, masked=True), carry)
    lse = m + jnp.log(l)
    o_low = (acc / l).astype(BF).astype(F32)
    delta = jnp.sum(do_f * o_low, axis=0, keepdims=True)

    def bwd(b, dq, masked):
        start = pl.multiple_of(b * QN, QN)
        k = kv_ref[pl.ds(start, QN), :]
        s = dot(k, q_t)
        p = jnp.exp(s - lse)
        if masked:
            p = jnp.where(k_place + (b % 4) * 256 <= q_place, p, 0.0)
        dp = dot(k, do_t)
        ds = (p * (dp - delta)).astype(BF)
        dkv_ref[pl.ds(start, QN), :] = (dot(ds, q0) + dot(p.astype(BF), do0)).astype(BF)
        return dq + dot(kt_ref[b], ds)

    dq = jnp.zeros((128, QN), F32)
    dq = lax.fori_loop(0, 4 * x, functools.partial(bwd, masked=False), dq)
    dq = lax.fori_loop(4 * x, 4 * x + 4, functools.partial(bwd, masked=True), dq)

    def blank(b, _):
        dkv_ref[pl.ds(pl.multiple_of(b * QN, QN), QN), :] = jnp.zeros((QN, 128), BF)
        return 0

    lax.fori_loop(4 * x + 4, NB, blank, 0)
    row = lax.broadcasted_iota(jnp.int32, (128, QN), 0)
    oq_ref[...] = jnp.where(row < HS, dq * HS ** (-0.5), o_low).T.astype(BF)


def attention(qd, kv):
    return pl.pallas_call(
        attn_kernel,
        grid=(GH,),
        in_specs=[
            pl.BlockSpec((QN, 128), lambda h: (0, h)),
            pl.BlockSpec((NB * QN, 128), lambda h: (0, h)),
        ],
        out_specs=[
            pl.BlockSpec((QN, 128), lambda h: (0, h)),
            pl.BlockSpec((NB * QN, 128), lambda h: (0, h)),
        ],
        out_shape=[
            jax.ShapeDtypeStruct((QN, GH * 128), BF),
            jax.ShapeDtypeStruct((NB * QN, GH * 128), BF),
        ],
        scratch_shapes=[pltpu.VMEM((NB, 128, QN), BF)],
        compiler_params=pltpu.CompilerParams(vmem_limit_bytes=50 * 1024 * 1024),
        cost_estimate=pl.CostEstimate(
            flops=3 * 7 * 2 * 512 * 8192 * 128, bytes_accessed=14000000, transcendentals=3 * 2 * 512 * 8192
        ),
    )(qd, kv)


def swap_cores(v):
    return lax.ppermute(v, "c", [(0, 1), (1, 0)])


def gather_packed(packed):
    mine = lax.all_to_all(jnp.broadcast_to(packed[None], (64,) + packed.shape), CHIPS, 0, 0)
    return mine, swap_cores(mine)


def scatter_sum(own_half, other_half):
    got = swap_cores(other_half)
    chip = (own_half.astype(F32) + got.astype(F32)).astype(BF)
    parts = lax.all_to_all(chip, CHIPS, 0, 0)
    return jnp.sum(parts.astype(F32), axis=0)


def halves(grad, width):
    rows = 6 * width // 128
    g = grad.reshape(2, 64, rows, 128)
    return g[0], g[1]


def local(
    tokens,
    first_gain,
    first_shift,
    second_gain,
    second_shift,
    qkv_weight,
    out_weight,
    up_weight,
    down_weight,
    cotangent,
):
    x = lax.axis_index("x")
    y = lax.axis_index("y")
    z = lax.axis_index("z")
    c = lax.axis_index("c")

    vecs = jnp.concatenate([first_gain, first_shift, second_gain, second_shift])
    vec_row = jnp.pad(vecs, (0, 16 * 128 - 24)).reshape(16, 128)
    pack_one = jnp.concatenate(
        [qkv_weight.reshape(108, 128), out_weight.reshape(36, 128), vec_row], axis=0
    )
    pack_two = jnp.concatenate([up_weight.reshape(144, 128), down_weight.reshape(144, 128)], axis=0)

    one_a, one_b = gather_packed(pack_one)

    def both(a, b, lo, hi):
        return jnp.stack([a[:, lo:hi], b[:, lo:hi]])

    qkv_full = both(one_a, one_b, 0, 108).reshape(D, 3 * D)
    out_full = both(one_a, one_b, 108, 144).reshape(D, D)
    vec_full = both(one_a, one_b, 144, 145)[:, :, 0, :24].reshape(2, 64, 4, 6)
    vec_full = jnp.transpose(vec_full, (2, 0, 1, 3)).reshape(4, D).astype(F32)

    place = jnp.arange(D, dtype=jnp.int32)
    core = jnp.where(place < D // 2, c, 1 - c)
    source = (place % (D // 2)) // 6 * 12 + core * 6 + place % 6
    perm = (jnp.arange(D, dtype=jnp.int32)[:, None] == source[None, :]).astype(BF)

    def to_gathered(v):
        return dot(v, perm).astype(BF)

    def from_gathered(v):
        return dot(v, perm, ((1,), (1,))).astype(BF)

    rows_f32 = to_gathered(tokens).astype(F32)
    cot_f32 = to_gathered(cotangent).astype(F32)
    first_norm, first_pull = jax.vjp(layer_norm, rows_f32, vec_full[0], vec_full[1])
    second_norm, second_pull = jax.vjp(layer_norm, rows_f32, vec_full[2], vec_full[3])
    first_low = first_norm.astype(BF)
    second_low = second_norm.astype(BF)

    row_first = (x * 8 + y * 4 + z) * 256 + c * 128
    lane = jnp.arange(3 * HS, dtype=jnp.int32)
    entry = lane % HS
    turned_lane = (entry < ROT) & (lane < 2 * HS)
    inverse = 1.0 / 10000.0 ** (2.0 * (entry % 8).astype(F32) / ROT)
    angles = (row_first + jnp.arange(128, dtype=jnp.int32)).astype(F32)[:, None] * inverse[None, :]
    cos_t = jnp.where(turned_lane, jnp.cos(angles), 1.0)
    sin_t = jnp.where(turned_lane, jnp.sin(angles), 0.0)
    sin_lo = jnp.where(entry < 8, sin_t, 0.0)
    sin_hi = jnp.where(entry >= 8, sin_t, 0.0)

    def rotate(v, sign):
        v = v.reshape(128, H, 3 * HS)
        ahead = jnp.roll(v, -8, axis=2)
        behind = jnp.roll(v, 8, axis=2)
        return v * cos_t[:, None] + sign * (behind * sin_hi[:, None] - ahead * sin_lo[:, None])

    turned = rotate(dot(first_low, qkv_full), 1.0)
    heads_grad = from_gathered(dot(cotangent, out_full, ((1,), (1,))).astype(BF))
    query = (turned[:, :, :HS] * HS ** (-0.5)).astype(BF)
    key_val = turned[:, :, HS:].astype(BF)
    query_grad_pair = jnp.concatenate([query, heads_grad.reshape(128, H, HS)], axis=2)
    send = jnp.concatenate(
        [query_grad_pair.reshape(128, 4, GH * 128), key_val.reshape(128, 4, GH * 128)], axis=2
    )
    got = lax.all_to_all(jnp.transpose(send, (1, 0, 2)), ("y", "c"), 0, 0).reshape(QN, 2 * GH * 128)
    qd = got[:, : GH * 128]
    kv = lax.all_gather(got[:, GH * 128 :], ("x", "z"), axis=0, tiled=True)

    two_a, two_b = gather_packed(pack_two)
    up_full = both(two_a, two_b, 0, 144).reshape(D, FF)
    down_a = two_a[:, 144:].reshape(64, 24, D)
    down_b = two_b[:, 144:].reshape(64, 24, D)
    down_full = jnp.stack(
        [jnp.where(c == 0, down_a, down_b), jnp.where(c == 0, down_b, down_a)], axis=1
    ).reshape(FF, D)
    hidden = dot(second_low, up_full)
    activated, gelu_pull = jax.vjp(exact_gelu, hidden)
    act_low = activated.astype(BF)
    feed_out = dot(act_low, down_full)
    act_grad = dot(cotangent, down_full, ((1,), (1,)))
    (hidden_grad,) = gelu_pull(act_grad)
    hidden_low = hidden_grad.astype(BF)
    up_w_grad = dot(second_low, hidden_low, ((0,), (0,))).astype(BF)
    down_w_grad = dot(act_low, cotangent, ((0,), (0,))).astype(BF)
    second_in = dot(hidden_low, up_full, ((1,), (1,)))
    second_rows, gain_two_grad, shift_two_grad = second_pull(second_in)

    oq, dkv = attention(qd, kv)
    oq = oq.reshape(QN, GH, 2, HS)
    dkv_mine = lax.psum_scatter(dkv, ("x", "z"), scatter_dimension=0, tiled=True)

    up_own, up_other = halves(up_w_grad, FF)
    down_g = down_w_grad.reshape(64, 2, 24, D)
    down_own = jnp.where(c == 0, down_g[:, 0], down_g[:, 1]).reshape(64, 144, 128)
    down_other = jnp.where(c == 0, down_g[:, 1], down_g[:, 0]).reshape(64, 144, 128)
    two_sum = scatter_sum(
        jnp.concatenate([up_own, down_own], axis=1), jnp.concatenate([up_other, down_other], axis=1)
    )
    up_out = two_sum[:144].reshape(6, FF)
    down_out = two_sum[144:].reshape(24, D)

    token_heads = lax.all_to_all(oq[:, :, 1].reshape(4, 128, GH * HS), ("y", "c"), 0, 0)
    token_heads = to_gathered(jnp.transpose(token_heads, (1, 0, 2)).reshape(128, D))
    attended = dot(token_heads, out_full)
    layer_out = (tokens.astype(F32) + attended + feed_out).astype(BF)
    out_w_grad = dot(token_heads, cotangent, ((0,), (0,))).astype(BF)

    assembled = jnp.concatenate(
        [oq[:, :, 0], dkv_mine.reshape(QN, GH, 2 * HS)], axis=2
    ).reshape(4, 128, GH * 3 * HS)
    back = lax.all_to_all(assembled, ("y", "c"), 0, 0)
    back = jnp.transpose(back, (1, 0, 2)).reshape(128, 3 * D)
    pre_low = rotate(back.astype(F32), -1.0).astype(BF).reshape(128, 3 * D)
    qkv_w_grad = dot(first_low, pre_low, ((0,), (0,))).astype(BF)
    first_in = dot(pre_low, qkv_full, ((1,), (1,)))
    first_rows, gain_one_grad, shift_one_grad = first_pull(first_in)
    tokens_grad = from_gathered((cot_f32 + first_rows + second_rows).astype(BF))

    vec_grad = jnp.stack([gain_one_grad, shift_one_grad, gain_two_grad, shift_two_grad]).astype(BF)
    vec_grad = jnp.transpose(vec_grad.reshape(4, 2, 64, 6), (1, 2, 0, 3)).reshape(2, 64, 24)
    vec_grad = jnp.pad(vec_grad, ((0, 0), (0, 0), (0, 16 * 128 - 24))).reshape(2, 64, 16, 128)
    qkv_own, qkv_other = halves(qkv_w_grad, 3 * D)
    out_own, out_other = halves(out_w_grad, D)
    one_sum = scatter_sum(
        jnp.concatenate([qkv_own, out_own, vec_grad[0]], axis=1),
        jnp.concatenate([qkv_other, out_other, vec_grad[1]], axis=1),
    )
    qkv_out = one_sum[:108].reshape(6, 3 * D)
    out_out = one_sum[108:144].reshape(6, D)
    vec_out = one_sum[144, :24].reshape(4, 6)
    return (
        layer_out,
        tokens_grad,
        vec_out[0],
        vec_out[1],
        vec_out[2],
        vec_out[3],
        qkv_out,
        out_out,
        up_out,
        down_out,
    )


def solution(mesh):
    fine = Mesh(mesh.devices.reshape(2, 4, 2, 4, 2), ALL)
    rows = P(ALL, None)
    vec = P(ALL)
    in_specs = (rows, vec, vec, vec, vec, rows, rows, rows, rows, rows)
    out_specs = (rows, rows, vec, vec, vec, vec, rows, rows, rows, rows)
    return jax.shard_map(local, mesh=fine, in_specs=in_specs, out_specs=out_specs, check_vma=False)
```

time: 2060 us -> 538 us (0.26)
  waiting for transfers between devices: 890 us -> 113 us
  blocking collectives: 476 us -> 132 us
  starting transfers between devices: 301 us -> 44.7 us
  matrix products: 184 us -> 29.1 us
  Pallas kernels: 0 us -> 41.5 us
  local copies, waits for them, and re-layouts: 137 us -> 110 us
    all_gather x5 -> x1, waiting for transfers between devices: 709 us -> 32.2 us  [local(): kv = lax.all_gather(got[:, GH * 128:], ('x', 'z'), axis=0, tiled=True)]
    unnamed x3 -> x0, blocking collectives: 459 us -> none
    unnamed x96 -> x0, starting transfers between devices: 300 us -> none
    dot_general x18 -> x15, matrix products: 164 us -> 29.1 us  [dot(): return lax.dot_general(a, b, (dims, ((), ())), preferred_element_type=F32)]
    reduce_scatter x2 -> x1, waiting for transfers between devices: 154 us -> 24.8 us  [local(): lax.psum_scatter(dkv, ('x', 'z'), scatter_dimension=0, tiled=True)]
    unnamed x275 -> x35, local copies, waits for them, and re-layouts: 121 us -> 3.1 us
    all_to_all x4 -> x3, blocking collectives: 16.6 us -> 132 us  [the longest x2 118 us: gather_packed(): lax.all_to_all(jnp.broadcast_to(packed[None], (64,) + packed.shape), CHIP...]
    all_to_all x0 -> x4, waiting for transfers between devices: none -> 55.9 us  [the longest x2 49.3 us: scatter_sum(): parts = lax.all_to_all(chip, CHIPS, 0, 0)]
  transfers between devices with their start and end apart: 103 -> 10, of which waited for: 14 -> 6; matrix products, arithmetic and copies ran while one was open for 33% -> 26% of each run, Pallas kernels for 0% -> 8%
where the time goes in v1:
time: 538 us; the launch traced here: 531 us
  blocking collectives  132 us (25%)
  waiting for transfers between devices  113 us (21%)
  local copies, waits for them, and re-layouts  110 us (20%)
  other arithmetic  45.4 us (8%)
  starting transfers between devices  44.7 us (8%)
  Pallas kernels  41.5 us (8%)
  matrix products  29.1 us (5%)
  between operations  15.2 us (3%)
    all_to_all x2, blocking collectives, gather_packed(): lax.all_to_all(jnp.broadcast_to(packed[None], (64,) + packed.shape), CHIP...  118 us
    all_to_all x2, waiting for transfers between devices, scatter_sum(): parts = lax.all_to_all(chip, CHIPS, 0, 0)  49.3 us
    pallas_call x1, Pallas kernels, attention(): pl.pallas_call(attn_kernel, grid=(GH,), in_specs=[pl.BlockSpec((QN, 128),...  41.5 us
    all_to_all x2, starting transfers between devices, scatter_sum(): parts = lax.all_to_all(chip, CHIPS, 0, 0)  37.3 us
    all_gather x1, waiting for transfers between devices, local(): kv = lax.all_gather(got[:, GH * 128:], ('x', 'z'), axis=0, tiled=True)  32.2 us
    dot_general x15, matrix products, dot(): return lax.dot_general(a, b, (dims, ((), ())), preferred_element_type=F32)  29.1 us
    reduce_scatter x1, waiting for transfers between devices, local(): lax.psum_scatter(dkv, ('x', 'z'), scatter_dimension=0, tiled=True)  24.8 us
    squeeze x6, local copies, waits for them, and re-layouts, halves(): return (g[0], g[1])  21.1 us
  transfers between devices with their start and end apart: 10, of which 6 were waited for; matrix products, arithmetic and copies ran while one was open for 26% of the time, Pallas kernels for 8%

profile of v1, /device:TPU:2, one launch (start us, length us, event | category | flops | bytes accessed | tf_op | source)
XLA Modules:
  0.0 530.9 jit_solution(1830770664984308423)
XLA Ops:
  10.0 47.4 %all_to_all.35 = bf16[64,160,128]{2,1,0:T(8,128)(2,1)S(1)} all-to-all(bf16[64,160,128]{2,1,0:T(8,128)(2,1)S(1)} %broadcast_in_dim.70), channel_id=1, replica_groups=mesh['dp'=2,'x'=4,'y'=2,'z'=4,'c'=2] {'dp','x','y','z'}, dimensions={0} | all-to-all | bytes 5242880 | tf_op jit(solution)/shard_map/all_to_all | solution.py:137
  57.4 2.5 copy.114
  61.4 0.9 slice.216
  62.5 1.1 slice_bitcast_fusion.5
  63.6 1.6 slice_bitcast_fusion.3
  66.8 1.6 slice_bitcast_fusion.2
  68.8 4.1 copy.120
  72.8 7.6 %reshape.468 = bf16[768,2304]{1,0:T(8,128)(2,1)} reshape(bf16[2,64,108,128]{3,2,1,0:T(8,128)(2,1)} %copy.120) | data formatting | bytes 7077888 | tf_op jit(solution)/shard_map/reshape | solution.py:183
  80.5 5.8 %copy.121 = bf16[2304,768]{1,0:T(8,128)(2,1)} copy(bf16[2304,768]{0,1:T(8,128)(2,1)} %bitcast.173) | data formatting | bytes 7077888 | tf_op jit(solution)/shard_map/dot_general | solution.py:37
  86.2 3.3 fusion.61
  90.8 1.1 slice_bitcast_fusion.4
  92.8 2.0 reshape.469
  94.8 2.7 fusion.47
  98.3 14.2 %all_to_all.36 = bf16[4,128,768]{2,1,0:T(8,128)(2,1)S(1)} all-to-all(bf16[4,128,768]{2,1,0:T(8,128)(2,1)S(1)} %maximum_bitcast_fusion), channel_id=1, replica_groups=mesh['dp'=2,'x'=4,'y'=2,'z'=4,'c'=2] {'y','c'}, dimensions={0} | all-to-all | bytes 1572864 | tf_op jit(solution)/shard_map/all_to_all | solution.py:231
  114.2 70.2 %all_to_all.37 = bf16[64,288,128]{2,1,0:T(8,128)(2,1)} all-to-all(bf16[64,288,128]{2,1,0:T(8,128)(2,1)S(1)} %broadcast_in_dim.76), channel_id=1, replica_groups=mesh['dp'=2,'x'=4,'y'=2,'z'=4,'c'=2] {'dp','x','y','z'}, dimensions={0} | all-to-all | bytes 9437184 | tf_op jit(solution)/shard_map/all_to_all | solution.py:137
  184.4 32.2 %all-gather.2.cloned.1.call-done.kv_ref = bf16[8192,384]{1,0:T(8,128)(2,1)} async-done(((bf16[512,384]{1,0:T(8,128)(2,1)}), bf16[8192,384]{1,0:T(8,128)(2,1)}) %all-gather.2.cloned.1.call-update) | async-done | bytes 6291472 | tf_op jit(solution)/shard_map/all_gather | solution.py:233
  216.5 41.5 %shard_map.177 = (bf16[512,384]{1,0:T(8,128)(2,1)S(1)}, bf16[8192,384]{1,0:T(8,128)(2,1)}) custom-call(bf16[512,384]{1,0:T(8,128)(2,1)S(1)} %get-tuple-element.49.qd_ref, bf16[8192,384]{1,0:T(8,128)(2,1)} %all-gather.2.cloned.1.call-done.kv_ref), custom_call_target="tpu_custom_call" | custom-call | flops 22548578304 | bytes 14000000 | tf_op jit(solution)/shard_map/pallas_call | solution.py:109
  258.6 6.7 %broadcast_select_fusion.3 = (bf16[64,144,128]{2,1,0:T(8,128)(2,1)}, bf16[64,144,128]{2,1,0:T(8,128)(2,1)}, bf16[1,64,144,128]{3,2,1,0:T(8,128)(2,1)}, bf16[1,64,144,128]{3,2,1,0:T(8,128)(2,1)}) fusion(pred[]{:T(512)S(6)} %eq.28, bf16[64,288,128]{2,1,0:T(8,128)(2,1)} %collective-permute-done.1, bf16[64,288,128]{2,1,0:T(8,128)(2,1)} %all_to_all.37), kind=kLoop, calls=%fused_computation.24 | loop fusion | flops 2359296 | bytes 18874368 | tf_op jit(solution)/shard_map/jit(_where)/select_n | solution.py:240
  265.3 5.4 %select_n.156 = bf16[64,1,24,768]{3,2,1,0:T(8,128)(2,1)} reshape(bf16[64,144,128]{2,1,0:T(8,128)(2,1)} %get-tuple-element.28) | data formatting | bytes 4718592 | tf_op jit(solution)/shard_map/jit(_where)/select_n | solution.py:240
  270.7 5.3 %select_n.158 = bf16[64,1,24,768]{3,2,1,0:T(8,128)(2,1)} reshape(bf16[64,144,128]{2,1,0:T(8,128)(2,1)} %get-tuple-element.29) | data formatting | bytes 4718592 | tf_op jit(solution)/shard_map/jit(_where)/select_n | solution.py:240
  276.0 5.0 pad_maximum_fusion
  281.0 8.4 %reshape.478 = bf16[768,3072]{1,0:T(8,128)(2,1)} reshape(bf16[2,64,144,128]{3,2,1,0:T(8,128)(2,1)} %pad_maximum_fusion) | data formatting | bytes 9437184 | tf_op jit(solution)/shard_map/reshape | solution.py:236
  289.4 2.9 pad_maximum_fusion.1
  293.1 4.1 multiply_convert_fusion
  297.3 1.9 add_convert_fusion.2
  299.2 1.4 convolution_convert_fusion.1
  300.6 2.5 fusion.99
  303.2 4.9 squeeze.55
  308.1 1.4 convolution_convert_fusion
  309.5 2.4 broadcast_select_fusion.1
  312.0 5.4 %select_n.163 = bf16[64,144,128]{2,1,0:T(8,128)(2,1)} reshape(bf16[64,1,24,768]{3,2,1,0:T(8,128)(2,1)} %get-tuple-element.33) | data formatting | bytes 4718592 | tf_op jit(solution)/shard_map/jit(_where)/select_n | solution.py:261
  317.3 4.8 pad_maximum_fusion.2
  322.4 4.1 fusion.110
  326.7 1.0 copy.136
  327.7 5.0 squeeze.54
  332.6 5.4 %select_n.161 = bf16[64,144,128]{2,1,0:T(8,128)(2,1)} reshape(bf16[64,1,24,768]{3,2,1,0:T(8,128)(2,1)} %get-tuple-element.32) | data formatting | bytes 4718592 | tf_op jit(solution)/shard_map/jit(_where)/select_n | solution.py:260
  339.0 3.4 all-to-all-start.2
  342.4 7.3 %add_convert_fusion = bf16[64,288,128]{2,1,0:T(8,128)(2,1)} fusion(bf16[64,288,128]{2,1,0:T(8,128)(2,1)} %collective-permute-done.3, bf16[64,144,128]{2,1,0:T(8,128)(2,1)} %select_n.161, bf16[64,144,128]{2,1,0:T(8,128)(2,1)} %squeeze.54), kind=kLoop, calls=%fused_computation.1 | loop fusion | flops 16515072 | bytes 14155776 | tf_op jit(solution)/shard_map/convert_element_type | solution.py:143
  350.3 24.8 %reduce-scatter.2.cloned.1.call-done = bf16[512,384]{1,0:T(8,128)(2,1)} async-done(((bf16[8192,384]{1,0:T(8,128)(2,1)}), bf16[512,384]{1,0:T(8,128)(2,1)}) %reduce-scatter.2.cloned.1.call-update) | async-done | bytes 393232 | tf_op jit(solution)/shard_map/reduce_scatter | solution.py:256
  375.1 1.2 copy.132
  376.5 0.9 copy.133
  377.4 3.5 all-to-all-start.4
  382.3 1.5 squeeze.48
  383.7 6.7 %all-to-all-done.4 = bf16[4,128,576]{1,2,0:T(8,128)(2,1)S(1)} async-done(((bf16[4,128,576]{1,2,0:T(8,128)(2,1)}), bf16[4,128,576]{1,2,0:T(8,128)(2,1)S(1)}, u32[]{:S(2)}, u32[]{:S(2)}) %all-to-all-start.4) | async-done | bytes 589856 | tf_op jit(solution)/shard_map/all_to_all | solution.py:277
  390.4 20.6 %all-to-all-start.6 = ((bf16[64,288,128]{2,1,0:T(8,128)(2,1)}), bf16[64,288,128]{2,1,0:T(8,128)(2,1)}, u32[]{:S(2)}, u32[]{:S(2)}) async-start(bf16[64,288,128]{2,1,0:T(8,128)(2,1)} %add_convert_fusion), calls=%async_computation.7 | async-start | bytes 9437184 | tf_op jit(solution)/shard_map/all_to_all | solution.py:144
  411.7 1.2 convolution_convert_fusion.2
  412.9 2.0 fusion.100
  415.0 1.2 copy-done.1
  416.2 1.3 fusion.111
  418.0 3.7 squeeze.47
  423.1 2.2 pad_slice_fusion.1
  425.3 2.3 copy.145
  427.6 3.0 pad_maximum_fusion.4
  430.7 2.4 squeeze.45
  433.1 3.7 squeeze.44
  436.7 2.3 copy.144
  439.1 3.4 add_convert_fusion.1
  442.5 29.2 %all-to-all-done.6 = bf16[64,288,128]{2,1,0:T(8,128)(2,1)} async-done(((bf16[64,288,128]{2,1,0:T(8,128)(2,1)}), bf16[64,288,128]{2,1,0:T(8,128)(2,1)}, u32[]{:S(2)}, u32[]{:S(2)}) %all-to-all-start.6) | async-done | bytes 4718624 | tf_op jit(solution)/shard_map/all_to_all | solution.py:144
  471.7 16.7 %all-to-all-start.5 = ((bf16[64,160,128]{2,1,0:T(8,128)(2,1)}), bf16[64,160,128]{2,1,0:T(8,128)(2,1)}, u32[]{:S(2)}, u32[]{:S(2)}) async-start(bf16[64,160,128]{2,1,0:T(8,128)(2,1)} %add_convert_fusion.1), calls=%async_computation.6 | async-start | bytes 5242880 | tf_op jit(solution)/shard_map/all_to_all | solution.py:144
  489.6 3.8 fusion.25
  493.5 3.0 convert_reduce_fusion
  497.8 1.9 fusion.49
  499.7 20.0 %all-to-all-done.5 = bf16[64,160,128]{2,1,0:T(8,128)(2,1)} async-done(((bf16[64,160,128]{2,1,0:T(8,128)(2,1)}), bf16[64,160,128]{2,1,0:T(8,128)(2,1)}, u32[]{:S(2)}, u32[]{:S(2)}) %all-to-all-start.5) | async-done | bytes 2621472 | tf_op jit(solution)/shard_map/all_to_all | solution.py:144
  519.7 2.1 convert_reduce_fusion.1
  (133 shorter events, 22.6 us)
Async XLA Ops:
  7.2 87.6 %copy-start = (bf16[128,768]{1,0:T(8,128)(2,1)S(1)}, bf16[128,768]{1,0:T(8,128)(2,1)}, u32[]{:S(2)}) copy-start(bf16[128,768]{1,0:T(8,128)(2,1)} %param.19) | copy-start | bytes 589828
  7.2 209.3 %all-gather.2.cloned.1.call-start = ((), (), s32[]{:S(2)}) async-start(), calls=%async_computation.8 | async-start | bytes 6684672 | tf_op jit(solution)/shard_map/all_gather | solution.py:233
  57.4 2.5 copy-start.4
  57.4 2.9 copy-start.12
  59.9 5.5 %collective-permute-start = (bf16[64,160,128]{2,0,1:T(8,128)(2,1)}, bf16[64,160,128]{2,0,1:T(8,128)(2,1)}, u32[]{:S(2)}, u32[]{:S(2)}) collective-permute-start(bf16[64,160,128]{2,0,1:T(8,128)(2,1)} %copy.114), channel_id=1, source_target_pairs={{0,1},{1,0},{2,3},{3,2},{4,5},{5,4},{6,7},{7,6},{8,9},{9,8},{10,11... | collective-permute-start | bytes 7864328 | tf_op jit(solution)/shard_map/ppermute | solution.py:133
  94.8 3.1 copy-start.9
  98.3 15.1 %copy-start.14 = (bf16[6,3072]{1,0:T(8,128)(2,1)S(1)}, bf16[6,3072]{1,0:T(8,128)(2,1)}, u32[]{:S(2)}) copy-start(bf16[6,3072]{1,0:T(8,128)(2,1)} %param.17) | copy-start | bytes 110596
  98.3 15.2 %copy-start.15 = (bf16[24,768]{1,0:T(8,128)(2,1)S(1)}, bf16[24,768]{1,0:T(8,128)(2,1)}, u32[]{:S(2)}) copy-start(bf16[24,768]{1,0:T(8,128)(2,1)} %param.18) | copy-start | bytes 110596
  113.3 261.8 %reduce-scatter.2.cloned.1.call-start = ((), (), s32[]{:S(2)}) async-start(), calls=%async_computation.9 | async-start | bytes 6684672 | tf_op jit(solution)/shard_map/reduce_scatter | solution.py:256
  184.4 74.2 %collective-permute-start.1 = (bf16[64,288,128]{2,1,0:T(8,128)(2,1)}, bf16[64,288,128]{2,1,0:T(8,128)(2,1)}, u32[]{:S(2)}, u32[]{:S(2)}) collective-permute-start(bf16[64,288,128]{2,1,0:T(8,128)(2,1)} %all_to_all.37), channel_id=1, source_target_pairs={{0,1},{1,0},{2,3},{3,2},{4,5},{5,4},{6,7},{7,6},{8,9},{9,8},{10,11... | collective-permute-start | bytes 14155784 | tf_op jit(solution)/shard_map/ppermute | solution.py:133
  289.4 3.8 copy-start.3
  293.1 4.1 copy-start.2
  297.3 10.8 %copy-start.5 = (bf16[128,3072]{1,0:T(8,128)(2,1)}, bf16[128,3072]{1,0:T(8,128)(2,1)S(1)}, u32[]{:S(2)}) copy-start(bf16[128,3072]{1,0:T(8,128)(2,1)S(1)} %get-tuple-element.26) | copy-start | bytes 2359300
  322.2 20.2 %collective-permute-start.3 = (bf16[64,288,128]{2,1,0:T(8,128)(2,1)}, bf16[64,288,128]{2,1,0:T(8,128)(2,1)}, u32[]{:S(2)}, u32[]{:S(2)}) collective-permute-start(bf16[64,288,128]{2,1,0:T(8,128)(2,1)} %pad_maximum_fusion.2), channel_id=1, source_target_pairs={{0,1},{1,0},{2,3},{3,2},{4,5},{5,4},{6,7},{7,6},{8,9},{9,8},{10,11... | collective-permute-start | bytes 14155784 | tf_op jit(solution)/shard_map/ppermute | solution.py:133
  339.0 10.7 %all-to-all-start.2 = ((bf16[4,128,192]{1,2,0:T(8,128)(2,1)}), bf16[4,128,192]{1,2,0:T(8,128)(2,1)S(1)}, u32[]{:S(2)}, u32[]{:S(2)}) async-start(bf16[4,128,192]{1,2,0:T(8,128)(2,1)} %copy.129), calls=%async_computation.2 | async-start | bytes 393216 | tf_op jit(solution)/shard_map/all_to_all | solution.py:268
  350.3 30.6 %copy-start.10 = (bf16[128,768]{1,0:T(8,128)(2,1)}, bf16[128,768]{1,0:T(8,128)(2,1)S(1)}, u32[]{:S(2)}) copy-start(bf16[128,768]{1,0:T(8,128)(2,1)S(1)} %fusion.48) | copy-start | bytes 589828
  377.4 13.0 %all-to-all-start.4 = ((bf16[4,128,576]{1,2,0:T(8,128)(2,1)}), bf16[4,128,576]{1,2,0:T(8,128)(2,1)S(1)}, u32[]{:S(2)}, u32[]{:S(2)}) async-start(bf16[4,128,576]{1,2,0:T(8,128)(2,1)} %copy.133), calls=%async_computation.5 | async-start | bytes 1179648 | tf_op jit(solution)/shard_map/all_to_all | solution.py:277
  390.4 81.4 %all-to-all-start.6 = ((bf16[64,288,128]{2,1,0:T(8,128)(2,1)}), bf16[64,288,128]{2,1,0:T(8,128)(2,1)}, u32[]{:S(2)}, u32[]{:S(2)}) async-start(bf16[64,288,128]{2,1,0:T(8,128)(2,1)} %add_convert_fusion), calls=%async_computation.7 | async-start | bytes 9437184 | tf_op jit(solution)/shard_map/all_to_all | solution.py:144
  412.9 3.3 copy-start.1
  418.0 3.7 copy-start.8
  430.7 8.4 %collective-permute-start.2 = (bf16[64,160,128]{2,1,0:T(8,128)(2,1)}, bf16[64,160,128]{2,1,0:T(8,128)(2,1)}, u32[]{:S(2)}, u32[]{:S(2)}) collective-permute-start(bf16[64,160,128]{2,1,0:T(8,128)(2,1)} %pad_maximum_fusion.4), channel_id=1, source_target_pairs={{0,1},{1,0},{2,3},{3,2},{4,5},{5,4},{6,7},{7,6},{8,9},{9,8},{10,11... | collective-permute-start | bytes 7864328 | tf_op jit(solution)/shard_map/ppermute | solution.py:133
  442.5 46.0 %copy-start.7 = (bf16[768,768]{1,0:T(8,128)(2,1)S(1)}, bf16[768,768]{1,0:T(8,128)(2,1)}, u32[]{:S(2)}) copy-start(bf16[768,768]{1,0:T(8,128)(2,1)} %reshape.469) | copy-start | bytes 3538948
  442.5 46.0 %copy-start.11 = (bf16[128,768]{1,0:T(8,128)(2,1)S(1)}, bf16[128,768]{1,0:T(8,128)(2,1)}, u32[]{:S(2)}) copy-start(bf16[128,768]{1,0:T(8,128)(2,1)} %copy-done.10) | copy-start | bytes 589828
  442.5 46.0 %copy-start.13 = (bf16[128,768]{1,0:T(8,128)(2,1)S(1)}, bf16[128,768]{1,0:T(8,128)(2,1)}, u32[]{:S(2)}) copy-start(bf16[128,768]{1,0:T(8,128)(2,1)} %param.10) | copy-start | bytes 589828
  471.7 48.0 %all-to-all-start.5 = ((bf16[64,160,128]{2,1,0:T(8,128)(2,1)}), bf16[64,160,128]{2,1,0:T(8,128)(2,1)}, u32[]{:S(2)}, u32[]{:S(2)}) async-start(bf16[64,160,128]{2,1,0:T(8,128)(2,1)} %add_convert_fusion.1), calls=%async_computation.6 | async-start | bytes 5242880 | tf_op jit(solution)/shard_map/all_to_all | solution.py:144
  488.5 1.1 copy-start.6
Sparse Core Ops, SparseCore 0:
  113.5 103.0 all-gather.1
  258.2 116.8 reduce-scatter.1
